TPU v7x, 256 devices: a whole 4x4x8 slice. The times are simulated.
256 devices in a mesh: dp: 2 (over core), fsdp: 8 (over z_lo, y), tensor: 16 (over z_hi, x).
Axes of the slice: x: 4, y: 4, z: 8 (z_hi: 4, z_lo: 2; z = z_hi * 2 + z_lo), core: 2. Of those that a mesh axis runs over, the one named last changes fastest.
Arguments:
- replica_grads: bfloat16 [2, 3584, 10240], P('dp', 'fsdp', 'tensor'), may hold values from -6 to 6
- basis_left: bfloat16 [3584, 3584], P('fsdp'), may hold values from -0.09375 to 0.09375
- basis_right: bfloat16 [10240, 10240], P('fsdp', 'tensor'), may hold values from -0.0625 to 0.0625
- first_moment: float32 [3584, 10240], P(('dp', 'fsdp'), 'tensor'), may hold values from -6 to 6
- second_moment: float32 [3584, 10240], P(('dp', 'fsdp'), 'tensor'), may hold values from 0.5 to 4
Outputs:
- first_next: float32 [3584, 10240], P(('dp', 'fsdp'), 'tensor')
- second_next: float32 [3584, 10240], P(('dp', 'fsdp'), 'tensor')
- update: float32 [3584, 10240], P('fsdp', 'tensor')
All inputs are finite; a program needn't handle non-finite values.
Results may differ from a plain program's by a relative error of at most 0.02.
Values may be sent and summed in bfloat16 or wider, within the bound.
A program may use at most 128 MiB of HBM per device.

v0:
```python
import jax
import jax.numpy as jnp
from jax import lax
from jax.sharding import PartitionSpec as P

ADAM_STEP = 10


beta_first = 0.9
beta_second = 0.95
epsilon = 1e-08


def per_device(replica_grads, basis_left, basis_right, first_moment, second_moment):
    summed = lax.psum_scatter(
        replica_grads[0].astype(jnp.float32).astype(jnp.bfloat16),
        "dp",
        scatter_dimension=0,
        tiled=True,
    )
    shard_rows = summed.shape[0]
    own_basis = lax.dynamic_slice_in_dim(
        basis_left, lax.axis_index("dp") * shard_rows, shard_rows, 0
    )
    rot_left = lax.psum_scatter(
        lax.dot_general(
            own_basis, summed, (((0,), (0,)), ((), ())), preferred_element_type=jnp.float32
        ).astype(jnp.bfloat16),
        ("dp", "fsdp"),
        scatter_dimension=0,
        tiled=True,
    )
    basis_full = lax.all_gather(basis_right, "fsdp", axis=0, tiled=True)
    basis_part = basis_full
    rotated = jnp.dot(
        lax.all_gather(rot_left, "tensor", axis=1, tiled=True),
        basis_part,
        preferred_element_type=jnp.float32,
    )
    first_next = beta_first * first_moment + (1.0 - beta_first) * rotated
    second_next = beta_second * second_moment + (1.0 - beta_second) * rotated * rotated
    first_hat = first_next / (1.0 - beta_first**ADAM_STEP)
    second_hat = second_next / (1.0 - beta_second**ADAM_STEP)
    direction = (first_hat / (jnp.sqrt(second_hat) + epsilon)).astype(jnp.bfloat16)
    basis_part = basis_full
    back_right = lax.psum_scatter(
        lax.dot_general(
            basis_part, direction, (((1,), (1,)), ((), ())), preferred_element_type=jnp.float32
        ).astype(jnp.bfloat16),
        "tensor",
        scatter_dimension=0,
        tiled=True,
    )
    gathered = lax.all_gather(back_right, ("dp", "fsdp"), axis=1, tiled=True)
    update = lax.dot_general(
        basis_left, gathered, (((1,), (1,)), ((), ())), preferred_element_type=jnp.float32
    )
    return (first_next, second_next, update)


def solution(mesh):
    placed = (
        P("dp", "fsdp", "tensor"),
        P("fsdp", None),
        P("fsdp", "tensor"),
        P(("dp", "fsdp"), "tensor"),
        P(("dp", "fsdp"), "tensor"),
    )
    return jax.shard_map(
        per_device,
        mesh=mesh,
        in_specs=placed,
        out_specs=(P(("dp", "fsdp"), "tensor"), P(("dp", "fsdp"), "tensor"), P("fsdp", "tensor")),
        check_vma=False,
    )
```

profile of v0, /device:TPU:1, one launch (start us, length us, event | category | flops | bytes accessed | tf_op | source)
XLA Modules:
  0.0 522.0 jit_solution(17860607751716990243)
XLA Ops:
  7.2 0.0 copy-start
  7.2 0.0 reduce-scatter.6.cloned.1.call-start
  7.2 0.7 reduce-scatter.6.cloned.1.call-update
  7.9 0.0 reduce-scatter.8.cloned.1.call-start
  8.0 20.5 %reduce-scatter.6.cloned.1.call-done = bf16[224,640]{1,0:T(8,128)(2,1)} async-done(((bf16[448,640]{1,0:T(8,128)(2,1)}), bf16[224,640]{1,0:T(8,128)(2,1)}) %reduce-scatter.6.cloned.1.call-update) | async-done | bytes 286736 | tf_op jit(solution)/shard_map/reduce_scatter | solution.py:15
  28.4 0.0 copy-done
  28.4 4.7 convolution_convert_fusion.1
  33.2 0.0 reduce-scatter.8.cloned.1.call-update
  33.2 0.0 all-gather.4.cloned.1.call-start
  33.2 78.3 %reduce-scatter.8.cloned.1.call-done = bf16[224,640]{1,0:T(8,128)(2,1)} async-done(((bf16[3584,640]{1,0:T(8,128)(2,1)}), bf16[224,640]{1,0:T(8,128)(2,1)}) %reduce-scatter.8.cloned.1.call-update) | async-done | bytes 286736 | tf_op jit(solution)/shard_map/reduce_scatter | solution.py:25
  111.6 0.0 all-gather.4.cloned.1.call-update
  111.6 0.0 all-gather.6.cloned.1.call-start
  111.6 0.5 all-gather.6.cloned.1.call-update
  112.2 0.0 reduce-scatter.10.cloned.1.call-start
  112.2 79.4 %all-gather.4.cloned.1.call-done = bf16[224,10240]{1,0:T(8,128)(2,1)} async-done(((bf16[224,640]{1,0:T(8,128)(2,1)}), bf16[224,10240]{1,0:T(8,128)(2,1)}) %all-gather.4.cloned.1.call-update) | async-done | bytes 4587536 | tf_op jit(solution)/shard_map/all_gather | solution.py:36
  191.6 145.5 %all-gather.6.cloned.1.call-done = bf16[10240,640]{1,0:T(8,128)(2,1)} async-done(((bf16[1280,640]{1,0:T(8,128)(2,1)}), bf16[10240,640]{1,0:T(8,128)(2,1)}) %all-gather.6.cloned.1.call-update) | async-done | bytes 13107216 | tf_op jit(solution)/shard_map/all_gather | solution.py:33
  337.1 11.0 %fusion.2 = (f32[224,640]{1,0:T(8,128)}, f32[224,640]{1,0:T(8,128)}) fusion(f32[224,640]{1,0:T(8,128)} %param.9, f32[224,640]{1,0:T(8,128)} %param.8, bf16[224,10240]{1,0:T(8,128)(2,1)} %all-gather.4.cloned.1.call-done, bf16[10240,640]{1,0:T(8,128)(2,1)} %all-gather.6.cloned.1.call-done), kind=kOutput, calls=%fused_computation.6 | convolution fusion | flops 2937016320 | bytes 19988480 | tf_op jit(solution)/shard_map/dot_general | solution.py:35
  348.1 11.6 %fusion = bf16[10240,224]{0,1:T(8,128)(2,1)} fusion(bf16[10240,640]{1,0:T(8,128)(2,1)} %all-gather.6.cloned.1.call-done, f32[224,640]{1,0:T(8,128)} %get-tuple-element.3, f32[224,640]{1,0:T(8,128)} %get-tuple-element.4), kind=kOutput, calls=%fused_computation.1 | convolution fusion | flops 2939023360 | bytes 18841600 | tf_op jit(solution)/shard_map/dot_general | solution.py:47
  359.7 7.5 %copy.8 = bf16[10240,224]{1,0:T(8,128)(2,1)} copy(bf16[10240,224]{0,1:T(8,128)(2,1)} %fusion) | data formatting | bytes 9175040
  367.2 0.0 reduce-scatter.10.cloned.1.call-update
  367.3 0.0 all-gather.8.cloned.1.call-start
  367.3 99.6 %reduce-scatter.10.cloned.1.call-done = bf16[640,224]{1,0:T(8,128)(2,1)} async-done(((bf16[10240,224]{1,0:T(8,128)(2,1)}), bf16[640,224]{1,0:T(8,128)(2,1)}) %reduce-scatter.10.cloned.1.call-update) | async-done | bytes 286736
  466.9 1.8 copy.9
  468.7 0.0 all-gather.8.cloned.1.call-update
  468.7 40.4 %all-gather.8.cloned.1.call-done = bf16[640,3584]{0,1:T(8,128)(2,1)} async-done(((bf16[640,224]{0,1:T(8,128)(2,1)}), bf16[640,3584]{0,1:T(8,128)(2,1)}) %all-gather.8.cloned.1.call-update) | async-done | bytes 4587536 | tf_op jit(solution)/shard_map/all_gather | solution.py:54
  509.2 5.9 %convolution_bitcast_fusion = f32[448,640]{1,0:T(8,128)} fusion(bf16[448,3584]{1,0:T(8,128)(2,1)S(1)} %copy-done, bf16[640,3584]{0,1:T(8,128)(2,1)} %all-gather.8.cloned.1.call-done), kind=kOutput, calls=%fused_computation.4 | convolution fusion | flops 2055208960 | bytes 8945664 | tf_op jit(solution)/shard_map/dot_general | solution.py:55
Async XLA Ops:
  7.2 21.3 %copy-start = (bf16[448,3584]{1,0:T(8,128)(2,1)S(1)}, bf16[448,3584]{1,0:T(8,128)(2,1)}, u32[]{:S(2)}) copy-start(bf16[448,3584]{1,0:T(8,128)(2,1)} %param.6) | copy-start | bytes 9633796
  7.2 21.3 %reduce-scatter.6.cloned.1.call-start = ((), (), s32[]{:S(2)}) async-start(), calls=%async_computation.3 | async-start | bytes 860160 | tf_op jit(solution)/shard_map/reduce_scatter | solution.py:15
  7.9 103.7 %reduce-scatter.8.cloned.1.call-start = ((), (), s32[]{:S(2)}) async-start(), calls=%async_computation.4 | async-start | bytes 4874240 | tf_op jit(solution)/shard_map/reduce_scatter | solution.py:25
  33.2 158.5 %all-gather.4.cloned.1.call-start = ((), (), s32[]{:S(2)}) async-start(), calls=%async_computation.5 | async-start | bytes 4874240 | tf_op jit(solution)/shard_map/all_gather | solution.py:36
  111.6 225.5 %all-gather.6.cloned.1.call-start = ((), (), s32[]{:S(2)}) async-start(), calls=%async_computation.6 | async-start | bytes 14745600 | tf_op jit(solution)/shard_map/all_gather | solution.py:33
  112.2 354.7 %reduce-scatter.10.cloned.1.call-start = ((), (), s32[]{:S(2)}) async-start(), calls=%async_computation.8 | async-start | bytes 5570560
  367.3 141.9 %all-gather.8.cloned.1.call-start = ((), (), s32[]{:S(2)}) async-start(), calls=%async_computation.7 | async-start | bytes 4874240 | tf_op jit(solution)/shard_map/all_gather | solution.py:54
Sparse Core Ops, SparseCore 0:
  10.5 17.8 reduce-scatter.5
  33.3 78.2 reduce-scatter.7
  114.4 77.2 all-gather.3
  193.4 143.6 all-gather.5
  367.4 99.4 reduce-scatter.9
  469.3 39.8 all-gather.7
where the time goes:
time: 522 us
  waiting for transfers between devices  465 us (89%)
  matrix products  33.3 us (6%)
  between operations  14.1 us (3%)
  local copies, waits for them, and re-layouts  9.37 us (2%)
    all_gather x1, waiting for transfers between devices, per_device(): basis_full = lax.all_gather(basis_right, 'fsdp', axis=0, tiled=True)  145 us
    unnamed x7, waiting for transfers between devices  101 us
    all_gather x1, waiting for transfers between devices, per_device(): lax.all_gather(rot_left, 'tensor', axis=1, tiled=True)  79.4 us
    reduce_scatter x1, waiting for transfers between devices, per_device(): lax.psum_scatter(lax.dot_general(own_basis, summed, (((0,), (0,)), ((), (...  78.3 us
    all_gather x1, waiting for transfers between devices, per_device(): gathered = lax.all_gather(back_right, ('dp', 'fsdp'), axis=1, tiled=True)  40.4 us
    reduce_scatter x1, waiting for transfers between devices, per_device(): lax.psum_scatter(replica_grads[0].astype(jnp.float32).astype(jnp.bfloat16...  20.5 us
    dot_general x1, matrix products, per_device(): lax.dot_general(basis_part, direction, (((1,), (1,)), ((), ())), preferre...  11.6 us
    dot_general x1, matrix products, per_device(): jnp.dot(lax.all_gather(rot_left, 'tensor', axis=1, tiled=True), basis_par...  11 us
  transfers between devices with their start and end apart: 6, of which 6 were waited for; matrix products, arithmetic and copies ran while one was open for 0% of the time, Pallas kernels for 0%

commit v1 on v0

v1 whole, which is shorter than its diff:
```python
import functools

import jax
import jax.numpy as jnp
from jax import lax
from jax.experimental import pallas as pl
from jax.experimental.pallas import tpu as pltpu
from jax.sharding import PartitionSpec as P

MESH = pl.DeviceIdType.MESH
F32 = jnp.float32
BF16 = jnp.bfloat16

ADAM_STEP = 10
beta_first = 0.9
beta_second = 0.95
epsilon = 1e-08

ROWS = 448
HALF = 224
COLS = 640
SUB = 112


class Ids:
    def __init__(self):
        self.table = {}
        self.count = 0

    def get(self, name, width=1):
        if name not in self.table:
            self.table[name] = self.count
            self.count += width
        return self.table[name]


def kernel(
    g_hbm, ql_hbm, qr_hbm, m1_hbm, m2_hbm,
    o1_hbm, o2_hbm, up_hbm,
    gv, gx, gs, G, Q, QL, T, Ts, Tr, Tb, Pb, Pr1, Pr2, Rs, Rf, Rr,
    m1, m2, o1, o2, D, B, Br1, Br2, Zr1, Zr2, br, brg, U, Ur,
    ssem, rsem, lsem,
):
    ids = Ids()
    c = lax.axis_index("dp")
    f = lax.axis_index("fsdp")
    t = lax.axis_index("tensor")
    zl, y = f // 4, f % 4
    zh, x = t // 4, t % 4
    p = x % 2
    is_a = c == p
    is_b = c != p
    oc = 1 - c
    yR, yL, yO = (y + 1) % 4, (y + 3) % 4, (y + 2) % 4
    xR, xL, xO = (x + 1) % 4, (x + 3) % 4, (x + 2) % 4
    zR, zL, zO = (zh + 1) % 4, (zh + 3) % 4, (zh + 2) % 4
    zlO = 1 - zl
    fO = zlO * 4 + y

    def dev(core=c, zl_=zl, y_=y, zh_=zh, x_=x):
        return (core, zl_ * 4 + y_, zh_ * 4 + x_)

    def rc(src, dst, sid, rid, device):
        return pltpu.make_async_remote_copy(
            src_ref=src, dst_ref=dst, send_sem=ssem.at[sid], recv_sem=rsem.at[rid],
            device_id=device, device_id_type=MESH,
        )

    common, in_a, in_b = [], [], []

    def send(to, build):
        build().start()
        to.append(build)

    def wait_recv(dst, rid):
        rc(dst, dst, 0, rid, dev(core=oc)).wait_recv()

    def half(h):
        return pl.ds(pl.multiple_of(h * HALF, 16), HALF)

    qr_load = pltpu.make_async_copy(
        qr_hbm.at[pl.ds(pl.multiple_of(c * COLS, COLS), COLS)], Q.at[f], lsem.at[0])
    g_load = pltpu.make_async_copy(g_hbm.at[0], gv, lsem.at[1])
    ql_load = pltpu.make_async_copy(ql_hbm, QL, lsem.at[2])
    m1_load = pltpu.make_async_copy(m1_hbm, m1, lsem.at[3])
    m2_load = pltpu.make_async_copy(m2_hbm, m2, lsem.at[4])
    g_load.start()
    qr_load.start()
    ql_load.start()
    m1_load.start()
    m2_load.start()

    barrier = pltpu.get_barrier_semaphore()
    friends = [dev(core=oc), dev(x_=xR), dev(x_=xL)]
    for core in (c, oc):
        friends += [dev(core=core, y_=yR), dev(core=core, y_=yL), dev(core=core, zl_=zlO),
                    dev(core=core, zh_=zR), dev(core=core, zh_=zL)]
    for friend in friends:
        pl.semaphore_signal(barrier, inc=1, device_id=friend, device_id_type=MESH)
    pl.semaphore_wait(barrier, len(friends))

    g_load.wait()
    send(common, lambda: rc(gv.at[half(oc)], gx, ids.get("g"), ids.get("g"), dev(core=oc)))
    qr_load.wait()

    def qpart(slot, a):
        return Q.at[slot, pl.ds(a * 320, 320)]

    def qsend(name, slot, a, device):
        i = ids.get(name)
        send(common, lambda: rc(qpart(slot, a), qpart(slot, a), i, i, device))

    for a in range(2):
        qsend(("Qy+", "own", a), f, a, dev(y_=yR))
        qsend(("Qy-", "own", a), f, a, dev(y_=yL))

    wait_recv(gx, ids.get("g"))
    gs[...] = (gv[half(c), :].astype(F32) + gx[...].astype(F32)).astype(BF16)

    own = 2 * zh + x // 2

    def gpart(slot, h):
        return G.at[slot, half(h)]

    gz_p, gz_m = ids.get("Gz+", 2), ids.get("Gz-", 2)
    send(common, lambda: rc(gs, gpart(own, c), gz_p + c, gz_p + c, dev(core=p, zh_=zR)))
    send(common, lambda: rc(gs, gpart(own, c), gz_m + c, gz_m + c, dev(core=p, zh_=zL)))
    for a in range(2):
        qsend(("Qz", a), f, a, dev(zl_=zlO))

    gx_p, gx_m = ids.get("Gx+", 8), ids.get("Gx-", 8)
    zq = [zh, zL, zR, zO]
    gf_p, gf_m = ids.get("Gxf+", 4), ids.get("Gxf-", 4)
    id_gs, id_zf_p, id_zf_m = ids.get("Gs"), ids.get("Gzf+"), ids.get("Gzf-")

    def gslot(q, x_):
        return 2 * zq[q] + x_ // 2

    def a_spread(q, h, src=None):
        for base, x_ in ((gx_p, xR), (gx_m, xL)):
            send(in_a, lambda base=base, x_=x_: rc(
                gpart(gslot(q, x), h) if src is None else src, gpart(gslot(q, x), h),
                base + 2 * q + h, base + 2 * q + h, dev(x_=x_)))

    def qy_own_forward():
        i = ids.get(("Qy+", "own", 0))
        wait_recv(qpart(zl * 4 + yL, 0), i)
        qsend(("Qyf+", "own"), zl * 4 + yL, 0, dev(y_=yR))
        i = ids.get(("Qy-", "own", 1))
        wait_recv(qpart(zl * 4 + yR, 1), i)
        qsend(("Qyf-", "own"), zl * 4 + yR, 1, dev(y_=yL))

    def qz_spread():
        for a in range(2):
            wait_recv(qpart(fO, a), ids.get(("Qz", a)))
            qsend(("Qy+", "par", a), fO, a, dev(y_=yR))
            qsend(("Qy-", "par", a), fO, a, dev(y_=yL))

    def qy_par_forward():
        wait_recv(qpart(zlO * 4 + yL, 0), ids.get(("Qy+", "par", 0)))
        qsend(("Qyf+", "par"), zlO * 4 + yL, 0, dev(y_=yR))
        wait_recv(qpart(zlO * 4 + yR, 1), ids.get(("Qy-", "par", 1)))
        qsend(("Qyf-", "par"), zlO * 4 + yR, 1, dev(y_=yL))

    @pl.when(is_a)
    def _():
        a_spread(0, c, src=gs)
        G[own, half(c), :] = gs[...]
        wait_recv(gpart(own, oc), id_gs)
        a_spread(0, oc)
        wait_recv(gpart(gslot(1, x), 0), gz_p + 0)
        send(in_a, lambda: rc(gpart(gslot(1, x), 0), gpart(gslot(1, x), 0), id_zf_p, id_zf_p, dev(zh_=zR)))
        a_spread(1, 0)
        wait_recv(gpart(gslot(2, x), 1), gz_m + 1)
        send(in_a, lambda: rc(gpart(gslot(2, x), 1), gpart(gslot(2, x), 1), id_zf_m, id_zf_m, dev(zh_=zL)))
        a_spread(2, 1)

    def b_forward(q, h):
        if h == 0:
            wait_recv(gpart(gslot(q, xL), 0), gx_p + 2 * q)
            send(in_b, lambda: rc(gpart(gslot(q, xL), 0), gpart(gslot(q, xL), 0), gf_p + q, gf_p + q, dev(x_=xR)))
        else:
            wait_recv(gpart(gslot(q, xR), 1), gx_m + 2 * q + 1)
            send(in_b, lambda: rc(gpart(gslot(q, xR), 1), gpart(gslot(q, xR), 1), gf_m + q, gf_m + q, dev(x_=xL)))

    @pl.when(is_b)
    def _():
        send(in_b, lambda: rc(gs, gpart(own, c), id_gs, id_gs, dev(core=oc)))
        b_forward(0, 0)
        b_forward(0, 1)

    qy_own_forward()
    qz_spread()

    @pl.when(is_a)
    def _():
        wait_recv(gpart(gslot(1, x), 1), gz_p + 1)
        a_spread(1, 1)
        wait_recv(gpart(gslot(2, x), 0), gz_m + 0)
        a_spread(2, 0)
        wait_recv(gpart(gslot(3, x), 0), id_zf_p)
        a_spread(3, 0)
        wait_recv(gpart(gslot(3, x), 1), id_zf_m)
        a_spread(3, 1)

    @pl.when(is_b)
    def _():
        b_forward(1, 0)
        b_forward(2, 1)
        b_forward(1, 1)
        b_forward(2, 0)

    qy_par_forward()

    @pl.when(is_b)
    def _():
        b_forward(3, 0)
        b_forward(3, 1)
        for q in range(4):
            wait_recv(gpart(gslot(q, xL), 1), gx_p + 2 * q + 1)
            wait_recv(gpart(gslot(q, xR), 0), gx_m + 2 * q)

    @pl.when(is_a)
    def _():
        for q in range(4):
            wait_recv(gpart(gslot(q, xO), 0), gf_p + q)
            wait_recv(gpart(gslot(q, xO), 1), gf_m + q)

    wait_recv(qpart(zl * 4 + yL, 1), ids.get(("Qy+", "own", 1)))
    wait_recv(qpart(zl * 4 + yR, 0), ids.get(("Qy-", "own", 0)))
    wait_recv(qpart(zlO * 4 + yL, 1), ids.get(("Qy+", "par", 1)))
    wait_recv(qpart(zlO * 4 + yR, 0), ids.get(("Qy-", "par", 0)))
    wait_recv(qpart(zl * 4 + yO, 0), ids.get(("Qyf+", "own")))
    wait_recv(qpart(zl * 4 + yO, 1), ids.get(("Qyf-", "own")))

    T[...] = jnp.zeros_like(T)
    last = zlO * 4 + yO

    @pl.loop(0, 7)
    def _(i):
        slot = (last + 1 + i) % 8
        T[...] += jnp.dot(G[slot], Q[slot], preferred_element_type=F32)

    wait_recv(qpart(last, 0), ids.get(("Qyf+", "par")))
    wait_recv(qpart(last, 1), ids.get(("Qyf-", "par")))
    T[...] += jnp.dot(G[last], Q[last], preferred_element_type=F32)

    Ts[...] = T[...].astype(BF16)
    id_t = ids.get("T")
    send(common, lambda: rc(Ts, Tr, id_t, id_t, dev(core=oc)))
    ql_load.wait()
    wait_recv(Tr, id_t)
    Tb[...] = (T[...] + Tr[...].astype(F32)).astype(BF16)

    for group in range(2):
        start = pl.multiple_of(c * 1792 + group * 896, 128)
        Pb[pl.ds(group * 896, 896), :] = lax.dot_general(
            QL[:, pl.ds(start, 896)], Tb[...], (((0,), (0,)), ((), ())), preferred_element_type=F32
        ).astype(BF16)

    def pblock(zl_, y_):
        return Pb.at[pl.ds(pl.multiple_of((zl_ * 4 + y_) * HALF, 16), HALF)]

    def psend(name, src, dst, device):
        i = ids.get(name)
        send(common, lambda: rc(src, dst, i, i, device))

    psend("Py1+", pblock(0, yO), Pr1.at[0], dev(y_=yR))
    psend("Py1-", pblock(1, yO), Pr1.at[1], dev(y_=yL))
    psend("Py2+n", pblock(1, yR), Pr2.at[0, 1], dev(y_=yR))
    psend("Py2-n", pblock(0, yL), Pr2.at[1, 0], dev(y_=yL))

    def add_into(dst, *others):
        total = dst[...].astype(F32)
        for other in others:
            total = total + other[...].astype(F32)
        dst[...] = total.astype(dst.dtype)

    wait_recv(Pr1.at[0], ids.get("Py1+"))
    add_into(pblock(0, yR), Pr1.at[0])
    psend("Py2+a", pblock(0, yR), Pr2.at[0, 0], dev(y_=yR))
    wait_recv(Pr1.at[1], ids.get("Py1-"))
    add_into(pblock(1, yL), Pr1.at[1])
    psend("Py2-a", pblock(1, yL), Pr2.at[1, 1], dev(y_=yL))
    wait_recv(Pr2.at[0, 1], ids.get("Py2+n"))
    wait_recv(Pr2.at[1, 0], ids.get("Py2-n"))
    wait_recv(Pr2.at[0, 0], ids.get("Py2+a"))
    wait_recv(Pr2.at[1, 1], ids.get("Py2-a"))

    def block_total(zl_):
        return (pblock(zl_, y)[...].astype(F32) + Pr2[0, zl_].astype(F32)
                + Pr2[1, zl_].astype(F32))

    Rs[...] = block_total(zlO).astype(BF16)
    psend("Pz", Rs, Rr, dev(zl_=zlO))
    Rf[...] = block_total(zl)
    m1_load.wait()
    m2_load.wait()
    wait_recv(Rr, ids.get("Pz"))

    @pl.loop(0, HALF // 32)
    def _(i):
        r = pl.ds(pl.multiple_of(i * 32, 32), 32)
        rotated = Rf[r, :] + Rr[r, :].astype(F32)
        first = beta_first * m1[r, :] + (1.0 - beta_first) * rotated
        second = beta_second * m2[r, :] + (1.0 - beta_second) * rotated * rotated
        o1[r, :] = first
        o2[r, :] = second
        first_hat = first / (1.0 - beta_first**ADAM_STEP)
        second_hat = second / (1.0 - beta_second**ADAM_STEP)
        D[c, r, :] = (first_hat / (jnp.sqrt(second_hat) + epsilon)).astype(BF16)

    id_d = ids.get("D")
    send(common, lambda: rc(D.at[c], D.at[c], id_d, id_d, dev(core=oc)))
    o1_store = pltpu.make_async_copy(o1, o1_hbm, lsem.at[5])
    o2_store = pltpu.make_async_copy(o2, o2_hbm, lsem.at[6])
    o1_store.start()
    o2_store.start()

    def multiply(xi, h):
        @pl.loop(0, 4)
        def _(z):
            B[xi * 4 + z, half(h), :] = lax.dot_general(
                D[h], Q[2 * z + xi], (((1,), (1,)), ((), ())), preferred_element_type=F32
            ).astype(BF16)

    def chunk_half(k):
        return (c + k // 2) % 2

    def rows(k):
        return pl.ds(pl.multiple_of(chunk_half(k) * HALF + (k % 2) * SUB, 16), SUB)

    b1_p, b1_m = ids.get("Bx1+", 4), ids.get("Bx1-", 4)
    b2n_p, b2n_m = ids.get("Bx2+n", 4), ids.get("Bx2-n", 4)
    b2a_p, b2a_m = ids.get("Bx2+a", 4), ids.get("Bx2-a", 4)
    z1_p, z1_m = ids.get("Bz1+", 4), ids.get("Bz1-", 4)
    z2_p, z2_m = ids.get("Bz2+", 4), ids.get("Bz2-", 4)
    fs_s, fz_s, fyp_s, fym_s = ids.get("Fs", 4), ids.get("Fz", 4), ids.get("Fy+", 4), ids.get("Fy-", 4)
    fpp, fpm = ids.get("Fyp+", 2), ids.get("Fyp-", 2)
    ffo_p, ffo_m, ffp_p, ffp_m = ids.get("Ff+o"), ids.get("Ff-o"), ids.get("Ff+p"), ids.get("Ff-p")

    def brpart(f_, s):
        return brg.at[pl.ds(pl.multiple_of(f_ * HALF + s * SUB, 16), SUB)]

    def f_spread(to, s):
        wait_recv(brpart(fO, s), fz_s + s)
        send(to, lambda: rc(brpart(fO, s), brpart(fO, s), fpp + s, fpp + s, dev(y_=yR)))
        send(to, lambda: rc(brpart(fO, s), brpart(fO, s), fpm + s, fpm + s, dev(y_=yL)))

    def f_forward_own(to, s):
        if s == 0:
            wait_recv(brpart(zl * 4 + yL, 0), fyp_s + 0)
            send(to, lambda: rc(brpart(zl * 4 + yL, 0), brpart(zl * 4 + yL, 0), ffo_p, ffo_p, dev(y_=yR)))
        else:
            wait_recv(brpart(zl * 4 + yR, 1), fym_s + 1)
            send(to, lambda: rc(brpart(zl * 4 + yR, 1), brpart(zl * 4 + yR, 1), ffo_m, ffo_m, dev(y_=yL)))

    def f_forward_partner(to, s):
        if s == 0:
            wait_recv(brpart(zlO * 4 + yL, 0), fpp + 0)
            send(to, lambda: rc(brpart(zlO * 4 + yL, 0), brpart(zlO * 4 + yL, 0), ffp_p, ffp_p, dev(y_=yR)))
        else:
            wait_recv(brpart(zlO * 4 + yR, 1), fpm + 1)
            send(to, lambda: rc(brpart(zlO * 4 + yR, 1), brpart(zlO * 4 + yR, 1), ffp_m, ffp_m, dev(y_=yL)))

    def add_blocks(first, count, r, terms):
        @pl.loop(0, count)
        def _(i):
            dst = B.at[first + i, r]
            total = dst[...].astype(F32)
            for term in terms(i):
                total = total + term[...].astype(F32)
            dst[...] = total.astype(BF16)

    @pl.when(is_a)
    def _():
        xi_own, xi_opp = x // 2, 1 - x // 2

        def opp_sends(k):
            def pair(first, base, x_):
                send(in_a, lambda: rc(B.at[pl.ds((1 - x // 2) * 4 + first, 2), rows(k)],
                                      Br1.at[pl.ds(first, 2), rows(k)], base + k, base + k, dev(x_=x_)))
            pair(0, b1_p, xR)
            pair(2, b1_m, xL)

        multiply(xi_opp, c)
        opp_sends(0)
        opp_sends(1)
        multiply(xi_own, c)
        wait_recv(D.at[oc], id_d)
        multiply(xi_opp, oc)
        opp_sends(2)
        opp_sends(3)
        multiply(xi_own, oc)

        def block(z_, k):
            return B.at[(x // 2) * 4 + z_, rows(k)]

        def reduce_chunk(k):
            r = rows(k)
            wait_recv(Br2.at[0, pl.ds(2, 2), r], b2n_p + k)
            wait_recv(Br2.at[1, pl.ds(0, 2), r], b2n_m + k)
            wait_recv(Br2.at[0, pl.ds(0, 2), r], b2a_p + k)
            wait_recv(Br2.at[1, pl.ds(2, 2), r], b2a_m + k)
            add_blocks(xi_own * 4, 4, r, lambda i: (Br2.at[0, i, r], Br2.at[1, i, r]))
            if k % 2 == 0:
                send(in_a, lambda: rc(block(zO, k), Zr1.at[rows(k)], z1_p + k, z1_p + k, dev(zh_=zR)))
                send(in_a, lambda: rc(block(zL, k), Zr2.at[1, rows(k)], z2_m + k, z2_m + k, dev(zh_=zL)))
                wait_recv(Zr1.at[r], z1_p + k)
                add_into(block(zR, k), Zr1.at[r])
                send(in_a, lambda: rc(block(zR, k), Zr2.at[0, rows(k)], z2_p + k, z2_p + k, dev(zh_=zR)))
            else:
                send(in_a, lambda: rc(block(zO, k), Zr1.at[rows(k)], z1_m + k, z1_m + k, dev(zh_=zL)))
                send(in_a, lambda: rc(block(zR, k), Zr2.at[0, rows(k)], z2_p + k, z2_p + k, dev(zh_=zR)))
                wait_recv(Zr1.at[r], z1_m + k)
                add_into(block(zL, k), Zr1.at[r])
                send(in_a, lambda: rc(block(zL, k), Zr2.at[1, rows(k)], z2_m + k, z2_m + k, dev(zh_=zL)))
            wait_recv(Zr2.at[0, r], z2_p + k)
            wait_recv(Zr2.at[1, r], z2_m + k)
            total = (block(zh, k)[...].astype(F32) + Zr2[0, r, :].astype(F32)
                     + Zr2[1, r, :].astype(F32)).astype(BF16)
            br[r, :] = total
            s = k % 2
            core = chunk_half(k)
            send(in_a, lambda: rc(br.at[rows(k)], brpart(f, s), fz_s + k, fz_s + s, dev(core=chunk_half(k), zl_=zlO)))
            send(in_a, lambda: rc(br.at[rows(k)], brpart(f, s), fyp_s + k, fyp_s + s, dev(core=chunk_half(k), y_=yR)))
            send(in_a, lambda: rc(br.at[rows(k)], brpart(f, s), fym_s + k, fym_s + s, dev(core=chunk_half(k), y_=yL)))
            if k < 2:
                brpart(f, s)[...] = total
            else:
                send(in_a, lambda: rc(br.at[rows(k)], brpart(f, s), fs_s + k, fs_s + s, dev(core=oc)))

        reduce_chunk(0)
        reduce_chunk(1)
        f_spread(in_a, 0)
        f_forward_own(in_a, 0)
        reduce_chunk(2)
        f_spread(in_a, 1)
        f_forward_own(in_a, 1)
        f_forward_partner(in_a, 0)
        reduce_chunk(3)
        f_forward_partner(in_a, 1)

    @pl.when(is_b)
    def _():
        xi_r, xi_l = xR // 2, xL // 2

        def x_send(first, xi_of, d, base, k, x_):
            send(in_b, lambda: rc(B.at[pl.ds(xi_of // 2 * 4 + first, 2), rows(k)],
                                  Br2.at[d, pl.ds(first, 2), rows(k)], base + k, base + k, dev(x_=x_)))

        def plain_sends(k):
            x_send(2, xR, 0, b2n_p, k, xR)
            x_send(0, xL, 1, b2n_m, k, xL)

        def sum_sends(k):
            r = rows(k)
            wait_recv(Br1.at[pl.ds(0, 2), r], b1_p + k)
            add_blocks(xi_r * 4, 2, r, lambda i: (Br1.at[i, r],))
            x_send(0, xR, 0, b2a_p, k, xR)
            wait_recv(Br1.at[pl.ds(2, 2), r], b1_m + k)
            add_blocks(xi_l * 4 + 2, 2, r, lambda i: (Br1.at[2 + i, r],))
            x_send(2, xL, 1, b2a_m, k, xL)

        multiply(0, c)
        multiply(1, c)
        plain_sends(0)
        plain_sends(1)
        wait_recv(D.at[oc], id_d)
        multiply(0, oc)
        multiply(1, oc)
        sum_sends(0)
        sum_sends(1)
        plain_sends(2)
        plain_sends(3)
        sum_sends(2)
        sum_sends(3)
        for s in range(2):
            f_spread(in_b, s)
            f_forward_own(in_b, s)
        for s in range(2):
            f_forward_partner(in_b, s)
        for s in range(2):
            wait_recv(brpart(f, s), fs_s + s)

    wait_recv(brpart(zl * 4 + yL, 1), fyp_s + 1)
    wait_recv(brpart(zl * 4 + yR, 0), fym_s + 0)
    wait_recv(brpart(zlO * 4 + yL, 1), fpp + 1)
    wait_recv(brpart(zlO * 4 + yR, 0), fpm + 0)
    wait_recv(brpart(zl * 4 + yO, 0), ffo_p)
    wait_recv(brpart(zl * 4 + yO, 1), ffo_m)
    wait_recv(brpart(zlO * 4 + yO, 0), ffp_p)
    wait_recv(brpart(zlO * 4 + yO, 1), ffp_m)

    start = pl.multiple_of(c * 1792, 128)
    U[...] = jnp.dot(QL[:, pl.ds(start, 896)], brg[pl.ds(0, 896), :], preferred_element_type=F32)
    start = pl.multiple_of(c * 1792 + 896, 128)
    U[...] += jnp.dot(QL[:, pl.ds(start, 896)], brg[pl.ds(896, 896), :], preferred_element_type=F32)
    id_u = ids.get("U")
    send(common, lambda: rc(U, Ur, id_u, id_u, dev(core=oc)))
    wait_recv(Ur, id_u)
    Ur[...] = Ur[...] + U[...]
    up_store = pltpu.make_async_copy(Ur, up_hbm, lsem.at[7])
    up_store.start()

    for build in common:
        build().wait_send()

    @pl.when(is_a)
    def _():
        for build in in_a:
            build().wait_send()

    @pl.when(is_b)
    def _():
        for build in in_b:
            build().wait_send()

    o1_store.wait()
    o2_store.wait()
    up_store.wait()
    assert ids.count <= SEMS, ids.count


SEMS = 160


def per_device(replica_grads, basis_left, basis_right, first_moment, second_moment):
    any_space = pl.BlockSpec(memory_space=pl.ANY)
    v = pltpu.VMEM
    scratch = [
        v((ROWS, COLS), BF16),
        v((HALF, COLS), BF16),
        v((HALF, COLS), BF16),
        v((8, ROWS, COLS), BF16),
        v((8, COLS, COLS), BF16),
        v((ROWS, 3584), BF16),
        v((ROWS, COLS), F32),
        v((ROWS, COLS), BF16),
        v((ROWS, COLS), BF16),
        v((ROWS, COLS), BF16),
        v((8 * HALF, COLS), BF16),
        v((2, HALF, COLS), BF16),
        v((2, 2, HALF, COLS), BF16),
        v((HALF, COLS), BF16),
        v((HALF, COLS), F32),
        v((HALF, COLS), BF16),
        v((HALF, COLS), F32),
        v((HALF, COLS), F32),
        v((HALF, COLS), F32),
        v((HALF, COLS), F32),
        v((2, HALF, COLS), BF16),
        v((8, ROWS, COLS), BF16),
        v((4, ROWS, COLS), BF16),
        v((2, 4, ROWS, COLS), BF16),
        v((ROWS, COLS), BF16),
        v((2, ROWS, COLS), BF16),
        v((ROWS, COLS), BF16),
        v((8 * HALF, COLS), BF16),
        v((ROWS, COLS), F32),
        v((ROWS, COLS), F32),
        pltpu.SemaphoreType.DMA((SEMS,)),
        pltpu.SemaphoreType.DMA((SEMS,)),
        pltpu.SemaphoreType.DMA((8,)),
    ]
    return pl.pallas_call(
        kernel,
        out_shape=(
            jax.ShapeDtypeStruct((HALF, COLS), F32),
            jax.ShapeDtypeStruct((HALF, COLS), F32),
            jax.ShapeDtypeStruct((ROWS, COLS), F32),
        ),
        in_specs=[any_space] * 5,
        out_specs=(any_space,) * 3,
        scratch_shapes=scratch,
        compiler_params=pltpu.CompilerParams(
            collective_id=0, has_side_effects=True, vmem_limit_bytes=60 * 2**20
        ),
        cost_estimate=pl.CostEstimate(
            flops=9 * 10**9, bytes_accessed=10 * 2**20, transcendentals=HALF * COLS
        ),
        name="soap_step",
    )(replica_grads, basis_left, basis_right, first_moment, second_moment)


def solution(mesh):
    placed = (
        P("dp", "fsdp", "tensor"),
        P("fsdp", None),
        P("fsdp", "tensor"),
        P(("dp", "fsdp"), "tensor"),
        P(("dp", "fsdp"), "tensor"),
    )
    return jax.shard_map(
        per_device,
        mesh=mesh,
        in_specs=placed,
        out_specs=(P(("dp", "fsdp"), "tensor"), P(("dp", "fsdp"), "tensor"), P("fsdp", "tensor")),
        check_vma=False,
    )
```

time: 522 us -> 199 us (0.38)
  waiting for transfers between devices: 465 us -> 0 us
  Pallas kernels: 0 us -> 193 us
  matrix products: 33.3 us -> 0 us
  between operations: 14.1 us -> 0.65 us
    all_gather x3 -> x0, waiting for transfers between devices: 265 us -> none  [the longest x1 145 us: per_device(): basis_full = lax.all_gather(basis_right, 'fsdp', axis=0, tiled=True)]
    pallas_call x0 -> x1, Pallas kernels: none -> 193 us  [per_device(): pl.pallas_call(kernel, out_shape=(jax.ShapeDtypeStruct((HALF, COLS), F32)...]
    unnamed x7 -> x0, waiting for transfers between devices: 101 us -> none
    reduce_scatter x2 -> x0, waiting for transfers between devices: 98.8 us -> none  [the longest x1 78.3 us: per_device(): lax.psum_scatter(lax.dot_general(own_basis, summed, (((0,), (0,)), ((), (...]
    dot_general x4 -> x0, matrix products: 33.3 us -> none  [the longest x1 11.6 us: per_device(): lax.dot_general(basis_part, direction, (((1,), (1,)), ((), ())), preferre...]
  transfers between devices with their start and end apart: 6 -> 0, of which waited for: 6 -> 0; matrix products, arithmetic and copies ran while one was open for 0% -> 0% of each run, Pallas kernels for 0% -> 0%
where the time goes in v1:
time: 199 us
  Pallas kernels  193 us (97%)
  local copies, waits for them, and re-layouts  4.91 us (2%)
    pallas_call x1, Pallas kernels, per_device(): pl.pallas_call(kernel, out_shape=(jax.ShapeDtypeStruct((HALF, COLS), F32)...  193 us
    unnamed x5, local copies, waits for them, and re-layouts  4.91 us

profile of v1, /device:TPU:1, one launch (start us, length us, event | category | flops | bytes accessed | tf_op | source)
XLA Modules:
  0.0 198.5 jit_solution(9786669024987757890)
XLA Ops:
  0.6 193.0 %soap_step.1 = (f32[224,640]{1,0:T(8,128)}, f32[224,640]{1,0:T(8,128)}, f32[448,640]{1,0:T(8,128)}) custom-call(bf16[1,448,640]{2,1,0:T(8,128)(2,1)} %g_hbm.1, bf16[448,3584]{1,0:T(8,128)(2,1)} %ql_hbm.1, bf16[1280,640]{1,0:T(8,128)(2,1)} %qr_hbm.1, f32[224,640]{1,0:T(8,128)} %m1_hbm.1, f32[224,640]{1,0:T(8,128)} %m2_hbm.1), custom_call_target="tpu_custom_call" | custom-call | flops 8999999488 | bytes 10485760 | tf_op jit(solution)/shard_map/soap_step/pallas_call | solution.py:566
  193.6 0.0 copy-start
  193.6 2.0 %copy.11 = f32[224,640]{1,0:T(8,128)} copy(f32[224,640]{1,0:T(8,128)} %get-tuple-element.6) | data formatting | bytes 1146880
  195.6 1.9 copy.12
  197.5 0.0 copy-done
  197.5 1.0 copy.13
Async XLA Ops:
  193.6 3.9 %copy-start = (f32[448,640]{1,0:T(8,128)S(1)}, f32[448,640]{1,0:T(8,128)}, u32[]{:S(2)}) copy-start(f32[448,640]{1,0:T(8,128)} %get-tuple-element.8) | copy-start | bytes 3440644

commit v2 on v1

v2 whole, which is shorter than its diff:
```python
import functools

import jax
import jax.numpy as jnp
from jax import lax
from jax.experimental import pallas as pl
from jax.experimental.pallas import tpu as pltpu
from jax.sharding import PartitionSpec as P

MESH = pl.DeviceIdType.MESH
F32 = jnp.float32
BF16 = jnp.bfloat16

ADAM_STEP = 10
beta_first = 0.9
beta_second = 0.95
epsilon = 1e-08

ROWS = 448
HALF = 224
COLS = 640
SUB = 112
YF = 384
WIDTHS = (128, 128, 128, 128, 128)


class Ids:
    def __init__(self):
        self.table = {}
        self.count = 0

    def get(self, name, width=1):
        if name not in self.table:
            self.table[name] = self.count
            self.count += width
        return self.table[name]


def kernel(
    g_hbm, ql_hbm, qr_hbm, m1_hbm, m2_hbm,
    rot_hbm, u_hbm,
    gv, gx, gs, G, Q, QL, QT, T, Ts, Tr, Tb, P0, P1, Pr1, Pr2, Rs, Rf, Rr, Zp, Sy1, Sy2,
    m1, m2, D, Bs, Br1s, Br2s, Zrs, brs, brgs, Us,
    ssem, rsem, lsem,
):
    ids = Ids()
    c = lax.axis_index("dp")
    f = lax.axis_index("fsdp")
    t = lax.axis_index("tensor")
    zl, y = f // 4, f % 4
    zh, x = t // 4, t % 4
    p = x % 2
    is_a = c == p
    is_b = c != p
    oc = 1 - c
    yR, yL, yO = (y + 1) % 4, (y + 3) % 4, (y + 2) % 4
    xR, xL, xO = (x + 1) % 4, (x + 3) % 4, (x + 2) % 4
    zR, zL, zO = (zh + 1) % 4, (zh + 3) % 4, (zh + 2) % 4
    zlO = 1 - zl
    fO = zlO * 4 + y

    def dev(core=c, zl_=zl, y_=y, zh_=zh, x_=x):
        return (core, zl_ * 4 + y_, zh_ * 4 + x_)

    def rc(src, dst, sid, rid, device):
        return pltpu.make_async_remote_copy(
            src_ref=src, dst_ref=dst, send_sem=ssem.at[sid], recv_sem=rsem.at[rid],
            device_id=device, device_id_type=MESH,
        )

    common, in_a, in_b = [], [], []

    def send(to, build):
        build().start()
        to.append(build)

    def wait_recv(dst, rid):
        rc(dst, dst, 0, rid, dev(core=oc)).wait_recv()

    def half(h):
        return pl.ds(pl.multiple_of(h * HALF, 16), HALF)

    qr_load = pltpu.make_async_copy(
        qr_hbm.at[pl.ds(pl.multiple_of(c * COLS, COLS), COLS)], Q.at[f], lsem.at[0])
    g_load = pltpu.make_async_copy(g_hbm.at[0], gv, lsem.at[1])
    ql_load = pltpu.make_async_copy(ql_hbm, QL, lsem.at[2])
    m1_load = pltpu.make_async_copy(m1_hbm, m1, lsem.at[3])
    m2_load = pltpu.make_async_copy(m2_hbm, m2, lsem.at[4])
    g_load.start()
    qr_load.start()
    ql_load.start()
    m1_load.start()
    m2_load.start()

    barrier = pltpu.get_barrier_semaphore()
    friends = [dev(core=oc), dev(x_=xR), dev(x_=xL)]
    for core in (c, oc):
        friends += [dev(core=core, y_=yR), dev(core=core, y_=yL), dev(core=core, zl_=zlO),
                    dev(core=core, zh_=zR), dev(core=core, zh_=zL)]
    for friend in friends:
        pl.semaphore_signal(barrier, inc=1, device_id=friend, device_id_type=MESH)
    pl.semaphore_wait(barrier, len(friends))

    g_load.wait()
    send(common, lambda: rc(gv.at[half(oc)], gx, ids.get("g"), ids.get("g"), dev(core=oc)))
    qr_load.wait()

    def qpart(slot, a):
        return Q.at[slot, pl.ds(a * 320, 320)]

    def qsend(name, slot, a, device):
        i = ids.get(name)
        send(common, lambda: rc(qpart(slot, a), qpart(slot, a), i, i, device))

    def qy_own(a):
        qsend(("Qy+", "own", a), f, a, dev(y_=yR))
        qsend(("Qy-", "own", a), f, a, dev(y_=yL))

    def qz_send(a):
        qsend(("Qz", a), f, a, dev(zl_=zlO))

    qy_own(0)
    qz_send(0)
    qy_own(1)

    wait_recv(gx, ids.get("g"))
    gs[...] = (gv[half(c), :].astype(F32) + gx[...].astype(F32)).astype(BF16)

    own = 2 * zh + x // 2

    def gpart(slot, h):
        return G.at[slot, half(h)]

    gz_p, gz_m = ids.get("Gz+", 2), ids.get("Gz-", 2)
    send(common, lambda: rc(gs, gpart(own, c), gz_p + c, gz_p + c, dev(core=p, zh_=zR)))
    send(common, lambda: rc(gs, gpart(own, c), gz_m + c, gz_m + c, dev(core=p, zh_=zL)))
    gx_p, gx_m = ids.get("Gx+", 8), ids.get("Gx-", 8)
    zq = [zh, zL, zR, zO]
    gf_p, gf_m = ids.get("Gxf+", 4), ids.get("Gxf-", 4)
    id_gs, id_zf_p, id_zf_m = ids.get("Gs"), ids.get("Gzf+"), ids.get("Gzf-")

    def gslot(q, x_):
        return 2 * zq[q] + x_ // 2

    def a_spread(q, h, src=None):
        for base, x_ in ((gx_p, xR), (gx_m, xL)):
            send(in_a, lambda base=base, x_=x_: rc(
                gpart(gslot(q, x), h) if src is None else src, gpart(gslot(q, x), h),
                base + 2 * q + h, base + 2 * q + h, dev(x_=x_)))

    def qy_own_forward():
        i = ids.get(("Qy+", "own", 0))
        wait_recv(qpart(zl * 4 + yL, 0), i)
        qsend(("Qyf+", "own"), zl * 4 + yL, 0, dev(y_=yR))
        i = ids.get(("Qy-", "own", 1))
        wait_recv(qpart(zl * 4 + yR, 1), i)
        qsend(("Qyf-", "own"), zl * 4 + yR, 1, dev(y_=yL))

    def qz_spread(a):
        wait_recv(qpart(fO, a), ids.get(("Qz", a)))
        qsend(("Qy+", "par", a), fO, a, dev(y_=yR))
        qsend(("Qy-", "par", a), fO, a, dev(y_=yL))

    def transpose_left(group):
        start = pl.multiple_of(c * 1792 + group * 896, 128)
        QT[pl.ds(group * 896, 896), :] = QL[:, pl.ds(start, 896)].T

    def qy_par_forward():
        wait_recv(qpart(zlO * 4 + yL, 0), ids.get(("Qy+", "par", 0)))
        qsend(("Qyf+", "par"), zlO * 4 + yL, 0, dev(y_=yR))
        wait_recv(qpart(zlO * 4 + yR, 1), ids.get(("Qy-", "par", 1)))
        qsend(("Qyf-", "par"), zlO * 4 + yR, 1, dev(y_=yL))

    def b_forward(q, h):
        if h == 0:
            wait_recv(gpart(gslot(q, xL), 0), gx_p + 2 * q)
            send(in_b, lambda: rc(gpart(gslot(q, xL), 0), gpart(gslot(q, xL), 0), gf_p + q, gf_p + q, dev(x_=xR)))
        else:
            wait_recv(gpart(gslot(q, xR), 1), gx_m + 2 * q + 1)
            send(in_b, lambda: rc(gpart(gslot(q, xR), 1), gpart(gslot(q, xR), 1), gf_m + q, gf_m + q, dev(x_=xL)))

    @pl.when(is_a)
    def _():
        a_spread(0, c, src=gs)
        G[own, half(c), :] = gs[...]
        wait_recv(gpart(own, oc), id_gs)
        a_spread(0, oc)
        wait_recv(gpart(gslot(1, x), 0), gz_p + 0)
        send(in_a, lambda: rc(gpart(gslot(1, x), 0), gpart(gslot(1, x), 0), id_zf_p, id_zf_p, dev(zh_=zR)))
        a_spread(1, 0)
        wait_recv(gpart(gslot(2, x), 1), gz_m + 1)
        send(in_a, lambda: rc(gpart(gslot(2, x), 1), gpart(gslot(2, x), 1), id_zf_m, id_zf_m, dev(zh_=zL)))
        a_spread(2, 1)

    @pl.when(is_b)
    def _():
        send(in_b, lambda: rc(gs, gpart(own, c), id_gs, id_gs, dev(core=oc)))
        b_forward(0, 0)
        b_forward(0, 1)

    qz_send(1)
    ql_load.wait()
    transpose_left(0)

    @pl.when(is_a)
    def _():
        wait_recv(gpart(gslot(1, x), 1), gz_p + 1)
        a_spread(1, 1)
        wait_recv(gpart(gslot(2, x), 0), gz_m + 0)
        a_spread(2, 0)

    qy_own_forward()

    @pl.when(is_a)
    def _():
        wait_recv(gpart(gslot(3, x), 0), id_zf_p)
        a_spread(3, 0)
        wait_recv(gpart(gslot(3, x), 1), id_zf_m)
        a_spread(3, 1)

    @pl.when(is_b)
    def _():
        b_forward(1, 0)
        b_forward(2, 1)

    qz_spread(0)

    @pl.when(is_b)
    def _():
        b_forward(1, 1)
        b_forward(2, 0)

    qz_spread(1)
    transpose_left(1)

    @pl.when(is_b)
    def _():
        b_forward(3, 0)
        b_forward(3, 1)

    qy_par_forward()

    @pl.when(is_b)
    def _():
        for q in range(4):
            wait_recv(gpart(gslot(q, xL), 1), gx_p + 2 * q + 1)
            wait_recv(gpart(gslot(q, xR), 0), gx_m + 2 * q)

    @pl.when(is_a)
    def _():
        for q in range(4):
            wait_recv(gpart(gslot(q, xO), 0), gf_p + q)
            wait_recv(gpart(gslot(q, xO), 1), gf_m + q)

    wait_recv(qpart(zl * 4 + yL, 1), ids.get(("Qy+", "own", 1)))
    wait_recv(qpart(zl * 4 + yR, 0), ids.get(("Qy-", "own", 0)))
    wait_recv(qpart(zlO * 4 + yL, 1), ids.get(("Qy+", "par", 1)))
    wait_recv(qpart(zlO * 4 + yR, 0), ids.get(("Qy-", "par", 0)))
    wait_recv(qpart(zl * 4 + yO, 0), ids.get(("Qyf+", "own")))
    wait_recv(qpart(zl * 4 + yO, 1), ids.get(("Qyf-", "own")))

    T[...] = jnp.zeros_like(T)
    last = zlO * 4 + yO

    @pl.loop(0, 7)
    def _(i):
        slot = (last + 1 + i) % 8
        T[...] += jnp.dot(G[slot], Q[slot], preferred_element_type=F32)

    wait_recv(qpart(last, 0), ids.get(("Qyf+", "par")))
    wait_recv(qpart(last, 1), ids.get(("Qyf-", "par")))
    T[...] += jnp.dot(G[last], Q[last], preferred_element_type=F32)

    Ts[...] = T[...].astype(BF16)
    id_t = ids.get("T")
    send(common, lambda: rc(Ts, Tr, id_t, id_t, dev(core=oc)))
    wait_recv(Tr, id_t)
    Tb[...] = (T[...] + Tr[...].astype(F32)).astype(BF16)

    def left(buf, group, lo, width):
        r = pl.ds(pl.multiple_of(group * 896, 128), 896)
        buf[r, :] = jnp.dot(
            QT[r, :], Tb[:, lo:lo + width], preferred_element_type=F32).astype(BF16)

    def pblock(buf, zl_, y_):
        return buf.at[pl.ds(pl.multiple_of((zl_ * 4 + y_) * HALF, 16), HALF)]

    def spart(y_, s):
        return P1.at[pl.ds(pl.multiple_of((zl * 4 + y_) * HALF + s * SUB, 16), SUB)]

    def half_of(buf, s):
        return buf.at[pl.ds(s * SUB, SUB)]

    def psend(name, src, dst, device):
        i = ids.get(name)
        send(common, lambda: rc(src, dst, i, i, device))

    def add_into(dst, *others):
        total = dst[...].astype(F32)
        for other in others:
            total = total + other[...].astype(F32)
        dst[...] = total.astype(dst.dtype)

    left(P1, zlO, YF, COLS - YF)
    for name, y_ in (("O", yO), ("R", yR), ("L", yL), ("S", y)):
        psend(("Pz1", name), pblock(P1, zlO, y_), Zp.at[y_], dev(zl_=zlO))
    left(P0, 0, 0, YF)
    psend("Py1+", pblock(P0, 0, yO), Pr1.at[0], dev(y_=yR))
    psend("Py2-n", pblock(P0, 0, yL), Pr2.at[1, 0], dev(y_=yL))
    left(P0, 1, 0, YF)
    psend("Py1-", pblock(P0, 1, yO), Pr1.at[1], dev(y_=yL))
    psend("Py2+n", pblock(P0, 1, yR), Pr2.at[0, 1], dev(y_=yR))
    left(P1, zl, YF, COLS - YF)

    def z_add(name, y_):
        wait_recv(Zp.at[y_], ids.get(("Pz1", name)))
        add_into(pblock(P1, zl, y_), Zp.at[y_])

    z_add("O", yO)
    psend("Sy1+", spart(yO, 0), Sy1.at[0], dev(y_=yR))
    psend("Sy1-", spart(yO, 1), Sy1.at[1], dev(y_=yL))
    wait_recv(Pr1.at[0], ids.get("Py1+"))
    add_into(pblock(P0, 0, yR), Pr1.at[0])
    psend("Py2+a", pblock(P0, 0, yR), Pr2.at[0, 0], dev(y_=yR))
    wait_recv(Pr1.at[1], ids.get("Py1-"))
    add_into(pblock(P0, 1, yL), Pr1.at[1])
    psend("Py2-a", pblock(P0, 1, yL), Pr2.at[1, 1], dev(y_=yL))
    z_add("R", yR)
    psend("Sy2+n", spart(yR, 1), half_of(Sy2.at[0], 1), dev(y_=yR))
    wait_recv(Sy1.at[0], ids.get("Sy1+"))
    add_into(spart(yR, 0), Sy1.at[0])
    psend("Sy2+a", spart(yR, 0), half_of(Sy2.at[0], 0), dev(y_=yR))
    z_add("L", yL)
    psend("Sy2-n", spart(yL, 0), half_of(Sy2.at[1], 0), dev(y_=yL))
    wait_recv(Sy1.at[1], ids.get("Sy1-"))
    add_into(spart(yL, 1), Sy1.at[1])
    psend("Sy2-a", spart(yL, 1), half_of(Sy2.at[1], 1), dev(y_=yL))
    wait_recv(Pr2.at[0, 1], ids.get("Py2+n"))
    wait_recv(Pr2.at[1, 0], ids.get("Py2-n"))
    wait_recv(Pr2.at[0, 0], ids.get("Py2+a"))
    wait_recv(Pr2.at[1, 1], ids.get("Py2-a"))

    def block_total(zl_):
        return (pblock(P0, zl_, y)[...].astype(F32) + Pr2[0, zl_].astype(F32)
                + Pr2[1, zl_].astype(F32))

    Rs[...] = block_total(zlO).astype(BF16)
    psend("Pz", Rs, Rr, dev(zl_=zlO))
    Rf[:, 0:YF] = block_total(zl)
    wait_recv(Zp.at[y], ids.get(("Pz1", "S")))
    total = pblock(P1, zl, y)[...].astype(F32) + Zp[y].astype(F32)
    wait_recv(half_of(Sy2.at[0], 0), ids.get("Sy2+a"))
    wait_recv(half_of(Sy2.at[0], 1), ids.get("Sy2+n"))
    wait_recv(half_of(Sy2.at[1], 0), ids.get("Sy2-n"))
    wait_recv(half_of(Sy2.at[1], 1), ids.get("Sy2-a"))
    Rf[:, YF:COLS] = total + Sy2[0].astype(F32) + Sy2[1].astype(F32)
    m1_load.wait()
    m2_load.wait()
    wait_recv(Rr, ids.get("Pz"))

    def adam(r, lo, hi, rotated):
        Rf[r, lo:hi] = rotated
        first = beta_first * m1[r, lo:hi] + (1.0 - beta_first) * rotated
        second = beta_second * m2[r, lo:hi] + (1.0 - beta_second) * rotated * rotated
        first_hat = first / (1.0 - beta_first**ADAM_STEP)
        second_hat = second / (1.0 - beta_second**ADAM_STEP)
        where = pl.ds(pl.multiple_of(c * HALF + r.start, 16), 32)
        D[where, lo:hi] = (first_hat / (jnp.sqrt(second_hat) + epsilon)).astype(BF16)

    @pl.loop(0, HALF // 32)
    def _(i):
        r = pl.ds(pl.multiple_of(i * 32, 32), 32)
        adam(r, 0, YF, Rf[r, 0:YF] + Rr[r, :].astype(F32))
        adam(r, YF, COLS, Rf[r, YF:COLS])

    id_d = ids.get("D")
    send(common, lambda: rc(D.at[half(c)], D.at[half(c)], id_d, id_d, dev(core=oc)))
    rot_store = pltpu.make_async_copy(Rf, rot_hbm, lsem.at[5])
    rot_store.start()
    wait_recv(D.at[half(oc)], id_d)

    chunks = range(len(WIDTHS))
    lows = [sum(WIDTHS[:k]) for k in chunks]
    n = len(WIDTHS)

    def multiply(k, xi):
        @pl.loop(0, 4)
        def _(z):
            Bs[k][xi * 4 + z] = lax.dot_general(
                D[...], Q[2 * z + xi, pl.ds(lows[k], WIDTHS[k])],
                (((1,), (1,)), ((), ())), preferred_element_type=F32
            ).astype(BF16)

    b1_p, b1_m = ids.get("Bx1+", n), ids.get("Bx1-", n)
    b2n_p, b2n_m = ids.get("Bx2+n", n), ids.get("Bx2-n", n)
    b2a_p, b2a_m = ids.get("Bx2+a", n), ids.get("Bx2-a", n)
    z_p, z_m, z_o = ids.get("Bz+", n), ids.get("Bz-", n), ids.get("Bzo", n)
    fs, fz = ids.get("Fs", n), ids.get("Fz", 2 * n)
    fy = [ids.get(("Fy", d), 2 * n) for d in range(3)]
    fp = [ids.get(("Fp", d), n) for d in range(3)]
    id_u = ids.get("U", n)

    ys = (yR, yL, yO)
    sources = (yL, yR, yO)

    def brrows(k, f_):
        return brgs[k].at[pl.ds(pl.multiple_of(f_ * HALF, 16), HALF)]

    def f_spread(to, k):
        wait_recv(brrows(k, fO), fz + k)
        for d in range(3):
            send(to, lambda d=d: rc(brrows(k, fO), brrows(k, fO), fp[d] + k, fp[d] + k, dev(y_=ys[d])))

    def final(k):
        for d in range(3):
            wait_recv(brrows(k, zl * 4 + sources[d]), fy[d] + k)
            wait_recv(brrows(k, zlO * 4 + sources[d]), fp[d] + k)
        start = pl.multiple_of(c * 1792, 128)
        Us[k][c] = jnp.dot(QL[:, pl.ds(start, 1792)], brgs[k][...], preferred_element_type=F32)

    def final_send(to, k):
        send(to, lambda: rc(Us[k].at[c], Us[k].at[c], id_u + k, id_u + k, dev(core=oc)))

    def u_store(k, core):
        return pltpu.make_async_copy(
            Us[k].at[core], u_hbm.at[core, :, pl.ds(lows[k], WIDTHS[k])], lsem.at[6 + 2 * k + core])

    def finish(k):
        u_store(k, c).start()
        wait_recv(Us[k].at[oc], id_u + k)
        u_store(k, oc).start()

    def add_blocks(buf, first, count, terms):
        @pl.loop(0, count)
        def _(i):
            dst = buf.at[first + i]
            total = dst[...].astype(F32)
            for term in terms(i):
                total = total + term[...].astype(F32)
            dst[...] = total.astype(BF16)

    @pl.when(is_a)
    def _():
        xi_own, xi_opp = x // 2, 1 - x // 2

        def opp_sends(k):
            send(in_a, lambda: rc(Bs[k].at[pl.ds((1 - x // 2) * 4, 2)], Br1s[k].at[pl.ds(0, 2)],
                                  b1_p + k, b1_p + k, dev(x_=xR)))
            send(in_a, lambda: rc(Bs[k].at[pl.ds((1 - x // 2) * 4 + 2, 2)], Br1s[k].at[pl.ds(2, 2)],
                                  b1_m + k, b1_m + k, dev(x_=xL)))

        def block(k, z_):
            return Bs[k].at[(x // 2) * 4 + z_]

        def x_total(k):
            wait_recv(Br2s[k].at[0, pl.ds(2, 2)], b2n_p + k)
            wait_recv(Br2s[k].at[1, pl.ds(0, 2)], b2n_m + k)
            wait_recv(Br2s[k].at[0, pl.ds(0, 2)], b2a_p + k)
            wait_recv(Br2s[k].at[1, pl.ds(2, 2)], b2a_m + k)
            add_blocks(Bs[k], xi_own * 4, 4, lambda i: (Br2s[k].at[0, i], Br2s[k].at[1, i]))
            send(in_a, lambda: rc(block(k, zR), Zrs[k].at[0], z_p + k, z_p + k, dev(zh_=zR)))
            send(in_a, lambda: rc(block(k, zL), Zrs[k].at[1], z_m + k, z_m + k, dev(zh_=zL)))
            send(in_a, lambda: rc(block(k, zO), Zrs[k].at[2], z_o + k, z_o + k, dev(zh_=zO)))

        def z_total(k):
            wait_recv(Zrs[k].at[0], z_p + k)
            wait_recv(Zrs[k].at[1], z_m + k)
            wait_recv(Zrs[k].at[2], z_o + k)
            brs[k][...] = (Bs[k][(x // 2) * 4 + zh].astype(F32) + Zrs[k][0].astype(F32)
                           + Zrs[k][1].astype(F32) + Zrs[k][2].astype(F32)).astype(BF16)
            for other in range(2):
                def src(other=other):
                    return brs[k].at[half(oc if other else c)]

                def to(other=other, **moved):
                    return dev(core=oc if other else c, **moved)

                send(in_a, lambda src=src, to=to, other=other: rc(
                    src(), brrows(k, f), fz + k + n * other, fz + k, to(zl_=zlO)))
                for d in range(3):
                    send(in_a, lambda src=src, to=to, other=other, d=d: rc(
                        src(), brrows(k, f), fy[d] + k + n * other, fy[d] + k, to(y_=ys[d])))
            send(in_a, lambda: rc(brs[k].at[half(oc)], brrows(k, f), fs + k, fs + k, dev(core=oc)))
            brrows(k, f)[...] = brs[k][half(c), :]

        def start_chunk(k):
            multiply(k, xi_opp)
            opp_sends(k)
            multiply(k, xi_own)

        start_chunk(0)
        start_chunk(1)
        for k in range(n + 4):
            if k < n:
                x_total(k)
            if k + 2 < n:
                start_chunk(k + 2)
            if 0 <= k - 1 < n:
                z_total(k - 1)
            if 0 <= k - 2 < n:
                f_spread(in_a, k - 2)
            if 0 <= k - 3 < n:
                final(k - 3)
                final_send(in_a, k - 3)
            if 0 <= k - 4 < n:
                finish(k - 4)

    @pl.when(is_b)
    def _():
        xi_r, xi_l = xR // 2, xL // 2

        def x_send(first, x_, d, base, k):
            send(in_b, lambda: rc(Bs[k].at[pl.ds(x_ // 2 * 4 + first, 2)],
                                  Br2s[k].at[d, pl.ds(first, 2)], base + k, base + k, dev(x_=x_)))

        def plain_sends(k):
            x_send(2, xR, 0, b2n_p, k)
            x_send(0, xL, 1, b2n_m, k)

        def sum_sends(k):
            wait_recv(Br1s[k].at[pl.ds(0, 2)], b1_p + k)
            add_blocks(Bs[k], xi_r * 4, 2, lambda i: (Br1s[k].at[i],))
            x_send(0, xR, 0, b2a_p, k)
            wait_recv(Br1s[k].at[pl.ds(2, 2)], b1_m + k)
            add_blocks(Bs[k], xi_l * 4 + 2, 2, lambda i: (Br1s[k].at[2 + i],))
            x_send(2, xL, 1, b2a_m, k)

        def start_chunk(k):
            multiply(k, 0)
            multiply(k, 1)

        start_chunk(0)
        plain_sends(0)
        start_chunk(1)
        for k in range(n + 5):
            if k < n:
                sum_sends(k)
            if k + 1 < n:
                plain_sends(k + 1)
            if k + 2 < n:
                start_chunk(k + 2)
            if 0 <= k - 3 < n:
                f_spread(in_b, k - 3)
            if 0 <= k - 4 < n:
                wait_recv(brrows(k - 4, f), fs + k - 4)
                final(k - 4)
                final_send(in_b, k - 4)
            if 0 <= k - 5 < n:
                finish(k - 5)

    for build in common:
        build().wait_send()

    @pl.when(is_a)
    def _():
        for build in in_a:
            build().wait_send()

    @pl.when(is_b)
    def _():
        for build in in_b:
            build().wait_send()

    rot_store.wait()
    for k in chunks:
        for core in range(2):
            u_store(k, core).wait()
    assert ids.count <= SEMS, ids.count


SEMS = 260


def per_device(replica_grads, basis_left, basis_right, first_moment, second_moment):
    any_space = pl.BlockSpec(memory_space=pl.ANY)
    v = pltpu.VMEM
    scratch = [
        v((ROWS, COLS), BF16),
        v((HALF, COLS), BF16),
        v((HALF, COLS), BF16),
        v((8, ROWS, COLS), BF16),
        v((8, COLS, COLS), BF16),
        v((ROWS, 3584), BF16),
        v((1792, ROWS), BF16),
        v((ROWS, COLS), F32),
        v((ROWS, COLS), BF16),
        v((ROWS, COLS), BF16),
        v((ROWS, COLS), BF16),
        v((8 * HALF, YF), BF16),
        v((8 * HALF, COLS - YF), BF16),
        v((2, HALF, YF), BF16),
        v((2, 2, HALF, YF), BF16),
        v((HALF, YF), BF16),
        v((HALF, COLS), F32),
        v((HALF, YF), BF16),
        v((4, HALF, COLS - YF), BF16),
        v((2, SUB, COLS - YF), BF16),
        v((2, HALF, COLS - YF), BF16),
        v((HALF, COLS), F32),
        v((HALF, COLS), F32),
        v((ROWS, COLS), BF16),
        [v((8, ROWS, w), BF16) for w in WIDTHS],
        [v((4, ROWS, w), BF16) for w in WIDTHS],
        [v((2, 4, ROWS, w), BF16) for w in WIDTHS],
        [v((3, ROWS, w), BF16) for w in WIDTHS],
        [v((ROWS, w), BF16) for w in WIDTHS],
        [v((8 * HALF, w), BF16) for w in WIDTHS],
        [v((2, ROWS, w), F32) for w in WIDTHS],
        pltpu.SemaphoreType.DMA((SEMS,)),
        pltpu.SemaphoreType.DMA((SEMS,)),
        pltpu.SemaphoreType.DMA((6 + 2 * len(WIDTHS),)),
    ]
    rotated, partials = pl.pallas_call(
        kernel,
        out_shape=(
            jax.ShapeDtypeStruct((HALF, COLS), F32),
            jax.ShapeDtypeStruct((2, ROWS, COLS), F32),
        ),
        in_specs=[any_space] * 5,
        out_specs=(any_space,) * 2,
        scratch_shapes=scratch,
        compiler_params=pltpu.CompilerParams(
            collective_id=0, has_side_effects=True, vmem_limit_bytes=60 * 2**20
        ),
        cost_estimate=pl.CostEstimate(
            flops=9 * 10**9, bytes_accessed=10 * 2**20, transcendentals=HALF * COLS
        ),
        name="soap_step",
    )(replica_grads, basis_left, basis_right, first_moment, second_moment)
    first_next = beta_first * first_moment + (1.0 - beta_first) * rotated
    second_next = beta_second * second_moment + (1.0 - beta_second) * rotated * rotated
    return (first_next, second_next, partials[0] + partials[1])


def solution(mesh):
    placed = (
        P("dp", "fsdp", "tensor"),
        P("fsdp", None),
        P("fsdp", "tensor"),
        P(("dp", "fsdp"), "tensor"),
        P(("dp", "fsdp"), "tensor"),
    )
    return jax.shard_map(
        per_device,
        mesh=mesh,
        in_specs=placed,
        out_specs=(P(("dp", "fsdp"), "tensor"), P(("dp", "fsdp"), "tensor"), P("fsdp", "tensor")),
        check_vma=False,
    )
```

time: 199 us -> 175 us (0.88)
  Pallas kernels: 193 us -> 171 us
  local copies, waits for them, and re-layouts: 4.91 us -> 0.01 us
  other arithmetic: 0 us -> 3.49 us
    pallas_call x1, Pallas kernels: 193 us -> 171 us  [per_device(): pl.pallas_call(kernel, out_shape=(jax.ShapeDtypeStruct((HALF, COLS), F32)...]
    unnamed x5 -> x6, local copies, waits for them, and re-layouts: 4.91 us -> 0.01 us
    add x0 -> x2, other arithmetic: none -> 3.49 us  [the longest x1 2.37 us: per_device(): beta_second * second_moment + (1.0 - beta_second) * rotated * rotated]
where the time goes in v2:
time: 175 us
  Pallas kernels  171 us (98%)
  other arithmetic  3.49 us (2%)
    pallas_call x1, Pallas kernels, per_device(): pl.pallas_call(kernel, out_shape=(jax.ShapeDtypeStruct((HALF, COLS), F32)...  171 us

profile of v2, /device:TPU:1, one launch (start us, length us, event | category | flops | bytes accessed | tf_op | source)
XLA Modules:
  0.0 175.0 jit_solution(17904043233611487097)
XLA Ops:
  0.6 0.0 copy-start.2
  0.6 0.0 copy-start.1
  0.7 170.8 %soap_step.1 = (f32[224,640]{1,0:T(8,128)}, f32[2,448,640]{2,1,0:T(8,128)}) custom-call(bf16[1,448,640]{2,1,0:T(8,128)(2,1)} %g_hbm.1, bf16[448,3584]{1,0:T(8,128)(2,1)} %ql_hbm.1, bf16[1280,640]{1,0:T(8,128)(2,1)} %qr_hbm.1, f32[224,640]{1,0:T(8,128)} %m1_hbm.1, f32[224,640]{1,0:T(8,128)} %m2_hbm.1), custom_call_target="tpu_custom_call" | custom-call | flops 8999999488 | bytes 10485760 | tf_op jit(solution)/shard_map/soap_step/pallas_call | solution.py:613
  171.5 0.0 copy-start
  171.5 0.0 copy-done.2
  171.5 0.0 copy-done.1
  171.5 2.4 %fusion = (f32[224,640]{1,0:T(8,128)}, f32[224,640]{1,0:T(8,128)}) fusion(f32[224,640]{1,0:T(8,128)} %get-tuple-element.5, f32[224,640]{1,0:T(8,128)S(1)} %copy-done.2, f32[224,640]{1,0:T(8,128)S(1)} %copy-done.1), kind=kLoop, calls=%fused_computation.2 | loop fusion | flops 1003520 | bytes 2867200 | tf_op jit(solution)/shard_map/add | solution.py:631
  173.9 0.0 copy-done
  173.9 1.1 add_bitcast_fusion
Async XLA Ops:
  0.6 170.9 %copy-start.2 = (f32[224,640]{1,0:T(8,128)S(1)}, f32[224,640]{1,0:T(8,128)}, u32[]{:S(2)}) copy-start(f32[224,640]{1,0:T(8,128)} %m2_hbm.1) | copy-start | bytes 1720324
  0.6 170.9 %copy-start.1 = (f32[224,640]{1,0:T(8,128)S(1)}, f32[224,640]{1,0:T(8,128)}, u32[]{:S(2)}) copy-start(f32[224,640]{1,0:T(8,128)} %m1_hbm.1) | copy-start | bytes 1720324
  171.5 2.4 %copy-start = (f32[2,448,640]{2,1,0:T(8,128)S(1)}, f32[2,448,640]{2,1,0:T(8,128)}, u32[]{:S(2)}) copy-start(f32[2,448,640]{2,1,0:T(8,128)} %get-tuple-element.6) | copy-start | bytes 6881284

commit v3 on v2

--- a/solution.py
+++ b/solution.py
@@ -39,7 +39,7 @@
 def kernel(
     g_hbm, ql_hbm, qr_hbm, m1_hbm, m2_hbm,
     rot_hbm, u_hbm,
-    gv, gx, gs, G, Q, QL, QT, T, Ts, Tr, Tb, P0, P1, Pr1, Pr2, Rs, Rf, Rr, Zp, Sy1, Sy2,
+    gv, gx, gs, Gq, G, Q, QL, QT, T, Tse, Tre, Tsl, Trl, Tb, P0, P1, Pr1, Pr2, Rs, Rf, Rr, Zp, Sy1, Sy2,
     m1, m2, D, Bs, Br1s, Br2s, Zrs, brs, brgs, Us,
     ssem, rsem, lsem,
 ):
@@ -93,9 +93,9 @@
     m2_load.start()
 
     barrier = pltpu.get_barrier_semaphore()
-    friends = [dev(core=oc), dev(x_=xR), dev(x_=xL)]
+    friends = [dev(core=oc), dev(zh_=zO)]
     for core in (c, oc):
-        friends += [dev(core=core, y_=yR), dev(core=core, y_=yL), dev(core=core, zl_=zlO),
+        friends += [dev(core=core, x_=xR), dev(core=core, x_=xL), dev(core=core, y_=yR), dev(core=core, y_=yL), dev(core=core, zl_=zlO),
                     dev(core=core, zh_=zR), dev(core=core, zh_=zL)]
     for friend in friends:
         pl.semaphore_signal(barrier, inc=1, device_id=friend, device_id_type=MESH)
@@ -131,13 +131,13 @@
     def gpart(slot, h):
         return G.at[slot, half(h)]
 
-    gz_p, gz_m = ids.get("Gz+", 2), ids.get("Gz-", 2)
+    gz_p, gz_m, gz_o = ids.get("Gz+", 2), ids.get("Gz-", 2), ids.get("Gzo", 2)
     send(common, lambda: rc(gs, gpart(own, c), gz_p + c, gz_p + c, dev(core=p, zh_=zR)))
     send(common, lambda: rc(gs, gpart(own, c), gz_m + c, gz_m + c, dev(core=p, zh_=zL)))
     gx_p, gx_m = ids.get("Gx+", 8), ids.get("Gx-", 8)
     zq = [zh, zL, zR, zO]
     gf_p, gf_m = ids.get("Gxf+", 4), ids.get("Gxf-", 4)
-    id_gs, id_zf_p, id_zf_m = ids.get("Gs"), ids.get("Gzf+"), ids.get("Gzf-")
+    id_gs, id_gs3 = ids.get("Gs"), ids.get("Gs3")
 
     def gslot(q, x_):
         return 2 * zq[q] + x_ // 2
@@ -147,6 +147,11 @@
             send(in_a, lambda base=base, x_=x_: rc(
                 gpart(gslot(q, x), h) if src is None else src, gpart(gslot(q, x), h),
                 base + 2 * q + h, base + 2 * q + h, dev(x_=x_)))
+
+    def b_spread(q, src):
+        for base, x_ in ((gx_p, xR), (gx_m, xL)):
+            send(in_b, lambda base=base, x_=x_: rc(
+                src, gpart(gslot(q, x), c), base + 2 * q + c, base + 2 * q + c, dev(core=oc, x_=x_)))
 
     def qy_own_forward():
         i = ids.get(("Qy+", "own", 0))
@@ -165,11 +170,21 @@
         start = pl.multiple_of(c * 1792 + group * 896, 128)
         QT[pl.ds(group * 896, 896), :] = QL[:, pl.ds(start, 896)].T
 
+    def qz_opposite():
+        wait_recv(qpart(zl * 4 + yO, 1), ids.get(("Qyf-", "own")))
+        i = ids.get("Qzo")
+        send(common, lambda: rc(qpart(zl * 4 + yO, 1), qpart(zl * 4 + yO, 1), i, i, dev(zl_=zlO)))
+
+    def quarter(slot, a):
+        return Q.at[slot, pl.ds(a * 160, 160)]
+
     def qy_par_forward():
         wait_recv(qpart(zlO * 4 + yL, 0), ids.get(("Qy+", "par", 0)))
-        qsend(("Qyf+", "par"), zlO * 4 + yL, 0, dev(y_=yR))
-        wait_recv(qpart(zlO * 4 + yR, 1), ids.get(("Qy-", "par", 1)))
-        qsend(("Qyf-", "par"), zlO * 4 + yR, 1, dev(y_=yL))
+        i = ids.get(("Qyf+", "par"))
+        send(common, lambda: rc(quarter(zlO * 4 + yL, 0), quarter(zlO * 4 + yL, 0), i, i, dev(y_=yR)))
+        wait_recv(qpart(zlO * 4 + yR, 0), ids.get(("Qy-", "par", 0)))
+        j = ids.get(("Qyf-", "par"))
+        send(common, lambda: rc(quarter(zlO * 4 + yR, 1), quarter(zlO * 4 + yR, 1), j, j, dev(y_=yL)))
 
     def b_forward(q, h):
         if h == 0:
@@ -181,19 +196,18 @@
 
     @pl.when(is_a)
     def _():
+        send(in_a, lambda: rc(gs, gpart(own, c), gz_o + c, gz_o + c, dev(zh_=zO)))
         a_spread(0, c, src=gs)
         G[own, half(c), :] = gs[...]
-        wait_recv(gpart(own, oc), id_gs)
-        a_spread(0, oc)
         wait_recv(gpart(gslot(1, x), 0), gz_p + 0)
-        send(in_a, lambda: rc(gpart(gslot(1, x), 0), gpart(gslot(1, x), 0), id_zf_p, id_zf_p, dev(zh_=zR)))
         a_spread(1, 0)
         wait_recv(gpart(gslot(2, x), 1), gz_m + 1)
-        send(in_a, lambda: rc(gpart(gslot(2, x), 1), gpart(gslot(2, x), 1), id_zf_m, id_zf_m, dev(zh_=zL)))
         a_spread(2, 1)
 
     @pl.when(is_b)
     def _():
+        send(in_b, lambda: rc(gs, Gq, gz_o + c, gz_o + c, dev(zh_=zO)))
+        b_spread(0, gs)
         send(in_b, lambda: rc(gs, gpart(own, c), id_gs, id_gs, dev(core=oc)))
         b_forward(0, 0)
         b_forward(0, 1)
@@ -213,14 +227,15 @@
 
     @pl.when(is_a)
     def _():
-        wait_recv(gpart(gslot(3, x), 0), id_zf_p)
-        a_spread(3, 0)
-        wait_recv(gpart(gslot(3, x), 1), id_zf_m)
-        a_spread(3, 1)
+        wait_recv(gpart(gslot(3, x), c), gz_o + c)
+        a_spread(3, c)
 
     @pl.when(is_b)
     def _():
         b_forward(1, 0)
+        wait_recv(Gq, gz_o + c)
+        b_spread(3, Gq)
+        send(in_b, lambda: rc(Gq, gpart(gslot(3, x), c), id_gs3, id_gs3, dev(core=oc)))
         b_forward(2, 1)
 
     qz_spread(0)
@@ -238,6 +253,7 @@
         b_forward(3, 0)
         b_forward(3, 1)
 
+    qz_opposite()
     qy_par_forward()
 
     @pl.when(is_b)
@@ -248,34 +264,50 @@
 
     @pl.when(is_a)
     def _():
+        wait_recv(gpart(own, oc), id_gs)
+        wait_recv(gpart(gslot(3, x), oc), id_gs3)
         for q in range(4):
             wait_recv(gpart(gslot(q, xO), 0), gf_p + q)
             wait_recv(gpart(gslot(q, xO), 1), gf_m + q)
 
+    def psend(name, src, dst, device):
+        i = ids.get(name)
+        send(common, lambda: rc(src, dst, i, i, device))
+
+    T[...] = jnp.zeros_like(T)
+    last = zlO * 4 + yO
+
+    def accumulate(slot):
+        T[...] += jnp.dot(G[slot], Q[slot], preferred_element_type=F32)
+
     wait_recv(qpart(zl * 4 + yL, 1), ids.get(("Qy+", "own", 1)))
     wait_recv(qpart(zl * 4 + yR, 0), ids.get(("Qy-", "own", 0)))
+    wait_recv(qpart(zl * 4 + yO, 0), ids.get(("Qyf+", "own")))
+
+    @pl.loop(0, 4)
+    def _(i):
+        accumulate(zl * 4 + i)
+
+    accumulate(fO)
     wait_recv(qpart(zlO * 4 + yL, 1), ids.get(("Qy+", "par", 1)))
-    wait_recv(qpart(zlO * 4 + yR, 0), ids.get(("Qy-", "par", 0)))
-    wait_recv(qpart(zl * 4 + yO, 0), ids.get(("Qyf+", "own")))
-    wait_recv(qpart(zl * 4 + yO, 1), ids.get(("Qyf-", "own")))
-
-    T[...] = jnp.zeros_like(T)
-    last = zlO * 4 + yO
-
-    @pl.loop(0, 7)
+    wait_recv(qpart(zlO * 4 + yR, 1), ids.get(("Qy-", "par", 1)))
+
+    @pl.loop(0, 2)
     def _(i):
-        slot = (last + 1 + i) % 8
-        T[...] += jnp.dot(G[slot], Q[slot], preferred_element_type=F32)
-
-    wait_recv(qpart(last, 0), ids.get(("Qyf+", "par")))
-    wait_recv(qpart(last, 1), ids.get(("Qyf-", "par")))
-    T[...] += jnp.dot(G[last], Q[last], preferred_element_type=F32)
-
-    Ts[...] = T[...].astype(BF16)
-    id_t = ids.get("T")
-    send(common, lambda: rc(Ts, Tr, id_t, id_t, dev(core=oc)))
-    wait_recv(Tr, id_t)
-    Tb[...] = (T[...] + Tr[...].astype(F32)).astype(BF16)
+        accumulate(zlO * 4 + (y + 1 + 2 * i) % 4)
+
+    wait_recv(quarter(last, 0), ids.get(("Qyf+", "par")))
+    wait_recv(quarter(last, 1), ids.get(("Qyf-", "par")))
+    wait_recv(qpart(last, 1), ids.get("Qzo"))
+    early, late = slice(YF, COLS), slice(0, YF)
+    for cols, buf, got, name in ((early, Tse, Tre, "Te"), (late, Tsl, Trl, "Tl")):
+        T[:, cols] += jnp.dot(G[last], Q[last, :, cols], preferred_element_type=F32)
+        buf[...] = T[:, cols].astype(BF16)
+        psend(name, buf, got, dev(core=oc))
+
+    def exchanged(got, cols, name):
+        wait_recv(got, ids.get(name))
+        Tb[:, cols] = (T[:, cols] + got[...].astype(F32)).astype(BF16)
 
     def left(buf, group, lo, width):
         r = pl.ds(pl.multiple_of(group * 896, 128), 896)
@@ -290,10 +322,6 @@
 
     def half_of(buf, s):
         return buf.at[pl.ds(s * SUB, SUB)]
-
-    def psend(name, src, dst, device):
-        i = ids.get(name)
-        send(common, lambda: rc(src, dst, i, i, device))
 
     def add_into(dst, *others):
         total = dst[...].astype(F32)
@@ -301,9 +329,11 @@
             total = total + other[...].astype(F32)
         dst[...] = total.astype(dst.dtype)
 
+    exchanged(Tre, early, "Te")
     left(P1, zlO, YF, COLS - YF)
     for name, y_ in (("O", yO), ("R", yR), ("L", yL), ("S", y)):
         psend(("Pz1", name), pblock(P1, zlO, y_), Zp.at[y_], dev(zl_=zlO))
+    exchanged(Trl, late, "Tl")
     left(P0, 0, 0, YF)
     psend("Py1+", pblock(P0, 0, yO), Pr1.at[0], dev(y_=yR))
     psend("Py2-n", pblock(P0, 0, yL), Pr2.at[1, 0], dev(y_=yL))
@@ -578,13 +608,16 @@
         v((ROWS, COLS), BF16),
         v((HALF, COLS), BF16),
         v((HALF, COLS), BF16),
+        v((HALF, COLS), BF16),
         v((8, ROWS, COLS), BF16),
         v((8, COLS, COLS), BF16),
         v((ROWS, 3584), BF16),
         v((1792, ROWS), BF16),
         v((ROWS, COLS), F32),
-        v((ROWS, COLS), BF16),
-        v((ROWS, COLS), BF16),
+        v((ROWS, COLS - YF), BF16),
+        v((ROWS, COLS - YF), BF16),
+        v((ROWS, YF), BF16),
+        v((ROWS, YF), BF16),
         v((ROWS, COLS), BF16),
         v((8 * HALF, YF), BF16),
         v((8 * HALF, COLS - YF), BF16),

time: 175 us -> 173 us (0.989)
  Pallas kernels: 171 us -> 169 us
where the time goes in v3:
time: 173 us
  Pallas kernels  169 us (98%)
  other arithmetic  3.49 us (2%)
    pallas_call x1, Pallas kernels, per_device(): pl.pallas_call(kernel, out_shape=(jax.ShapeDtypeStruct((HALF, COLS), F32)...  169 us

profile of v3, /device:TPU:1, one launch (start us, length us, event | category | flops | bytes accessed | tf_op | source)
XLA Modules:
  0.0 173.3 jit_solution(13938744395603824488)
XLA Ops:
  0.6 0.0 copy-start.2
  0.6 0.0 copy-start.1
  0.7 169.1 %soap_step.1 = (f32[224,640]{1,0:T(8,128)}, f32[2,448,640]{2,1,0:T(8,128)}) custom-call(bf16[1,448,640]{2,1,0:T(8,128)(2,1)} %g_hbm.1, bf16[448,3584]{1,0:T(8,128)(2,1)} %ql_hbm.1, bf16[1280,640]{1,0:T(8,128)(2,1)} %qr_hbm.1, f32[224,640]{1,0:T(8,128)} %m1_hbm.1, f32[224,640]{1,0:T(8,128)} %m2_hbm.1), custom_call_target="tpu_custom_call" | custom-call | flops 8999999488 | bytes 10485760 | tf_op jit(solution)/shard_map/soap_step/pallas_call | solution.py:646
  169.7 0.0 copy-start
  169.8 0.0 copy-done.2
  169.8 0.0 copy-done.1
  169.8 2.4 %fusion = (f32[224,640]{1,0:T(8,128)}, f32[224,640]{1,0:T(8,128)}) fusion(f32[224,640]{1,0:T(8,128)} %get-tuple-element.5, f32[224,640]{1,0:T(8,128)S(1)} %copy-done.2, f32[224,640]{1,0:T(8,128)S(1)} %copy-done.1), kind=kLoop, calls=%fused_computation.2 | loop fusion | flops 1003520 | bytes 2867200 | tf_op jit(solution)/shard_map/add | solution.py:664
  172.1 0.0 copy-done
  172.2 1.1 add_bitcast_fusion
Async XLA Ops:
  0.6 169.1 %copy-start.2 = (f32[224,640]{1,0:T(8,128)S(1)}, f32[224,640]{1,0:T(8,128)}, u32[]{:S(2)}) copy-start(f32[224,640]{1,0:T(8,128)} %m2_hbm.1) | copy-start | bytes 1720324
  0.6 169.1 %copy-start.1 = (f32[224,640]{1,0:T(8,128)S(1)}, f32[224,640]{1,0:T(8,128)}, u32[]{:S(2)}) copy-start(f32[224,640]{1,0:T(8,128)} %m1_hbm.1) | copy-start | bytes 1720324
  169.7 2.4 %copy-start = (f32[2,448,640]{2,1,0:T(8,128)S(1)}, f32[2,448,640]{2,1,0:T(8,128)}, u32[]{:S(2)}) copy-start(f32[2,448,640]{2,1,0:T(8,128)} %get-tuple-element.6) | copy-start | bytes 6881284

commit v4 on v3

--- a/solution.py
+++ b/solution.py
@@ -520,13 +520,14 @@
 
         start_chunk(0)
         start_chunk(1)
+        start_chunk(2)
         for k in range(n + 4):
             if k < n:
                 x_total(k)
-            if k + 2 < n:
-                start_chunk(k + 2)
             if 0 <= k - 1 < n:
                 z_total(k - 1)
+            if k + 3 < n:
+                start_chunk(k + 3)
             if 0 <= k - 2 < n:
                 f_spread(in_a, k - 2)
             if 0 <= k - 3 < n:

time: 173 us -> 171 us (0.988)
  Pallas kernels: 169 us -> 166 us
    pallas_call x1, Pallas kernels: 169 us -> 166 us  [per_device(): pl.pallas_call(kernel, out_shape=(jax.ShapeDtypeStruct((HALF, COLS), F32)...]
where the time goes in v4:
time: 171 us
  Pallas kernels  166 us (97%)
  other arithmetic  3.49 us (2%)
    pallas_call x1, Pallas kernels, per_device(): pl.pallas_call(kernel, out_shape=(jax.ShapeDtypeStruct((HALF, COLS), F32)...  166 us

profile of v4, /device:TPU:1, one launch (start us, length us, event | category | flops | bytes accessed | tf_op | source)
XLA Modules:
  0.0 170.6 jit_solution(18344929407027524566)
XLA Ops:
  0.6 0.0 copy-start.2
  0.6 0.0 copy-start.1
  0.7 166.4 %soap_step.1 = (f32[224,640]{1,0:T(8,128)}, f32[2,448,640]{2,1,0:T(8,128)}) custom-call(bf16[1,448,640]{2,1,0:T(8,128)(2,1)} %g_hbm.1, bf16[448,3584]{1,0:T(8,128)(2,1)} %ql_hbm.1, bf16[1280,640]{1,0:T(8,128)(2,1)} %qr_hbm.1, f32[224,640]{1,0:T(8,128)} %m1_hbm.1, f32[224,640]{1,0:T(8,128)} %m2_hbm.1), custom_call_target="tpu_custom_call" | custom-call | flops 8999999488 | bytes 10485760 | tf_op jit(solution)/shard_map/soap_step/pallas_call | solution.py:647
  167.1 0.0 copy-start
  167.1 0.0 copy-done.2
  167.1 0.0 copy-done.1
  167.1 2.4 %fusion = (f32[224,640]{1,0:T(8,128)}, f32[224,640]{1,0:T(8,128)}) fusion(f32[224,640]{1,0:T(8,128)} %get-tuple-element.5, f32[224,640]{1,0:T(8,128)S(1)} %copy-done.2, f32[224,640]{1,0:T(8,128)S(1)} %copy-done.1), kind=kLoop, calls=%fused_computation.2 | loop fusion | flops 1003520 | bytes 2867200 | tf_op jit(solution)/shard_map/add | solution.py:665
  169.5 0.0 copy-done
  169.5 1.1 add_bitcast_fusion
Async XLA Ops:
  0.6 166.4 %copy-start.2 = (f32[224,640]{1,0:T(8,128)S(1)}, f32[224,640]{1,0:T(8,128)}, u32[]{:S(2)}) copy-start(f32[224,640]{1,0:T(8,128)} %m2_hbm.1) | copy-start | bytes 1720324
  0.6 166.4 %copy-start.1 = (f32[224,640]{1,0:T(8,128)S(1)}, f32[224,640]{1,0:T(8,128)}, u32[]{:S(2)}) copy-start(f32[224,640]{1,0:T(8,128)} %m1_hbm.1) | copy-start | bytes 1720324
  167.1 2.4 %copy-start = (f32[2,448,640]{2,1,0:T(8,128)S(1)}, f32[2,448,640]{2,1,0:T(8,128)}, u32[]{:S(2)}) copy-start(f32[2,448,640]{2,1,0:T(8,128)} %get-tuple-element.6) | copy-start | bytes 6881284

commit v5 on v4

--- a/solution.py
+++ b/solution.py
@@ -563,13 +563,14 @@
         start_chunk(0)
         plain_sends(0)
         start_chunk(1)
+        start_chunk(2)
         for k in range(n + 5):
             if k < n:
                 sum_sends(k)
             if k + 1 < n:
                 plain_sends(k + 1)
-            if k + 2 < n:
-                start_chunk(k + 2)
+            if k + 3 < n:
+                start_chunk(k + 3)
             if 0 <= k - 3 < n:
                 f_spread(in_b, k - 3)
             if 0 <= k - 4 < n:

time: 171 us -> 171 us (level)
  no operation moved by 1% of the time
where the time goes in v5:
time: 171 us
  Pallas kernels  166 us (97%)
  other arithmetic  3.49 us (2%)
    pallas_call x1, Pallas kernels, per_device(): pl.pallas_call(kernel, out_shape=(jax.ShapeDtypeStruct((HALF, COLS), F32)...  166 us

profile of v5, /device:TPU:1, one launch (start us, length us, event | category | flops | bytes accessed | tf_op | source)
XLA Modules:
  0.0 170.6 jit_solution(8245491898896272079)
XLA Ops:
  0.6 0.0 copy-start.2
  0.6 0.0 copy-start.1
  0.7 166.4 %soap_step.1 = (f32[224,640]{1,0:T(8,128)}, f32[2,448,640]{2,1,0:T(8,128)}) custom-call(bf16[1,448,640]{2,1,0:T(8,128)(2,1)} %g_hbm.1, bf16[448,3584]{1,0:T(8,128)(2,1)} %ql_hbm.1, bf16[1280,640]{1,0:T(8,128)(2,1)} %qr_hbm.1, f32[224,640]{1,0:T(8,128)} %m1_hbm.1, f32[224,640]{1,0:T(8,128)} %m2_hbm.1), custom_call_target="tpu_custom_call" | custom-call | flops 8999999488 | bytes 10485760 | tf_op jit(solution)/shard_map/soap_step/pallas_call | solution.py:648
  167.1 0.0 copy-start
  167.1 0.0 copy-done.2
  167.1 0.0 copy-done.1
  167.1 2.4 %fusion = (f32[224,640]{1,0:T(8,128)}, f32[224,640]{1,0:T(8,128)}) fusion(f32[224,640]{1,0:T(8,128)} %get-tuple-element.5, f32[224,640]{1,0:T(8,128)S(1)} %copy-done.2, f32[224,640]{1,0:T(8,128)S(1)} %copy-done.1), kind=kLoop, calls=%fused_computation.2 | loop fusion | flops 1003520 | bytes 2867200 | tf_op jit(solution)/shard_map/add | solution.py:666
  169.5 0.0 copy-done
  169.5 1.1 add_bitcast_fusion
Async XLA Ops:
  0.6 166.4 %copy-start.2 = (f32[224,640]{1,0:T(8,128)S(1)}, f32[224,640]{1,0:T(8,128)}, u32[]{:S(2)}) copy-start(f32[224,640]{1,0:T(8,128)} %m2_hbm.1) | copy-start | bytes 1720324
  0.6 166.4 %copy-start.1 = (f32[224,640]{1,0:T(8,128)S(1)}, f32[224,640]{1,0:T(8,128)}, u32[]{:S(2)}) copy-start(f32[224,640]{1,0:T(8,128)} %m1_hbm.1) | copy-start | bytes 1720324
  167.1 2.4 %copy-start = (f32[2,448,640]{2,1,0:T(8,128)S(1)}, f32[2,448,640]{2,1,0:T(8,128)}, u32[]{:S(2)}) copy-start(f32[2,448,640]{2,1,0:T(8,128)} %get-tuple-element.6) | copy-start | bytes 6881284
